TPU v7x, 32 devices: a whole 2x2x4 slice. The times are simulated.
32 devices in a mesh: section: 8 (over y, x, core), peer: 4 (over z).
Axes of the slice: x: 2, y: 2, z: 4, core: 2. Of those that a mesh axis runs over, the one named last changes fastest.
Arguments:
- stash: bfloat16 [8, 4, 3, 8, 5120], P('section', 'peer'), may hold values from -134 to 134
- back_in: bfloat16 [8, 4, 3, 8, 5120], P('section', 'peer'), may hold values from -6 to 6
- down_proj: bfloat16 [8, 144, 5120], P('section'), may hold values from -0.078125 to 0.078125
- up_proj: bfloat16 [8, 144, 5120], P('section'), may hold values from -0.5 to 0.5
- gain: float32 [8, 5120], P('section'), may hold values from 0.5 to 1.5
- sent_to: int32 [8, 4, 3], P('section', 'peer'), may hold values from 0 to 3, as said below
- sent_count: int32 [8, 4], P('section', 'peer'), may hold values from 2 to 3, as said below
- recv_from: int32 [8, 4, 3], P('section', 'peer'), may hold values from 0 to 3, as said below
- back_live: int32 [8, 4, 3], P('section', 'peer'), may hold values from 0 to 1, as said below
Outputs:
- returned: bfloat16 [8, 4, 3, 8, 5120], P('section', 'peer')
- grad_down: bfloat16 [8, 144, 5120], P('section')
- grad_up: bfloat16 [8, 144, 5120], P('section')
Inputs may be any that keep to these rules, and one draw needn't show every extreme that they name: `sent_to`: the 3 slots of one device name distinct peers. `sent_count`: uneven over peers; on every section some peer has 3. `recv_from`: the 3 slots of one device name distinct peers. Peer c of section s - 1 (the last section before section 0) names peer a of section s in one of its first sent_count slots exactly when some slot of recv_from at (s, a) names c with back_live 1. `back_live`: on every section some device has all 3 slots live.
All inputs are finite; a program needn't handle non-finite values.
Results may differ from a plain program's by a relative error of at most 0.028.
Values may be sent and summed in bfloat16 or wider, within the bound.
A program may use at most 64 MiB of HBM per device.

v0:
```python
import jax
import jax.numpy as jnp
from jax import lax
from jax.sharding import PartitionSpec as P

epsilon = 1e-05


def passed_along(block, axis, distance):
    devices = range(lax.axis_size(axis))
    route = [((i - distance) % len(devices), i) for i in devices]
    return lax.ppermute(block, axis, route)


def compact(blocks, targets, live_count):
    peer_count = blocks.shape[0]
    send_slots = targets.shape[0]
    peer_index = jnp.arange(peer_count, dtype=jnp.int32)
    slot_index = jnp.arange(send_slots, dtype=jnp.int32)
    selector = (
        (targets[:, None] == peer_index[None, :]) & (slot_index[:, None] < live_count)
    ).astype(jnp.bfloat16)
    flat = blocks.reshape(peer_count, -1)
    packed = jnp.dot(selector, flat, preferred_element_type=jnp.float32).astype(jnp.bfloat16)
    return packed.reshape((send_slots,) + blocks.shape[1:])


def on_device(stash, back_in, down_proj, up_proj, gain, sent_to, sent_count, recv_from, back_live):
    peer_count = lax.axis_size("peer")
    live_slots = back_live[0, 0]
    slot_mask = live_slots.astype(jnp.bfloat16)[:, None, None]
    slot_count = stash.shape[2]
    micro_rows = stash.shape[3]
    model_width = stash.shape[4]
    stored = (stash[0, 0] * slot_mask).reshape(slot_count * micro_rows, model_width)
    incoming = (back_in[0, 0] * slot_mask).reshape(slot_count * micro_rows, model_width)
    section_gain = gain[0]
    down_local = down_proj[0]
    up_local = up_proj[0]
    stored_f = stored.astype(jnp.float32)
    inverse = lax.rsqrt(jnp.mean(stored_f * stored_f, axis=-1, keepdims=True) + epsilon)
    unit_rows = stored_f * inverse
    normed = (unit_rows * section_gain).astype(jnp.bfloat16)
    contract_last = (((1,), (1,)), ((), ()))
    contract_rows = (((0,), (0,)), ((), ()))
    preact = lax.dot_general(normed, down_local, contract_last, preferred_element_type=jnp.float32)
    sigmoid_pre = jax.nn.sigmoid(preact)
    activation = (preact * sigmoid_pre).astype(jnp.bfloat16)
    back_act = lax.dot_general(
        incoming, up_local, contract_last, preferred_element_type=jnp.float32
    )
    back_pre = (back_act * (sigmoid_pre * (1.0 + preact * (1.0 - sigmoid_pre)))).astype(
        jnp.bfloat16
    )
    back_norm = jnp.dot(back_pre, down_local, preferred_element_type=jnp.float32) * section_gain
    input_grad = incoming.astype(jnp.float32) + inverse * (
        back_norm - unit_rows * jnp.mean(back_norm * unit_rows, axis=-1, keepdims=True)
    )
    input_grad = input_grad.astype(jnp.bfloat16)
    peer_index = jnp.arange(peer_count, dtype=jnp.int32)
    spreader = (
        (recv_from[0, 0][None, :] == peer_index[:, None]) & (live_slots[None, :] == 1)
    ).astype(jnp.bfloat16)
    by_sender = jnp.dot(
        spreader, input_grad.reshape(slot_count, -1), preferred_element_type=jnp.float32
    ).astype(jnp.bfloat16)
    by_sender = by_sender.reshape(peer_count, micro_rows, model_width)
    exchanged = lax.all_to_all(by_sender, "peer", split_axis=0, concat_axis=0, tiled=True)
    arrived = passed_along(exchanged, "section", -1)
    returned = compact(arrived, sent_to[0, 0], sent_count[0, 0])
    part_down = (
        lax.dot_general(back_pre, normed, contract_rows, preferred_element_type=jnp.float32)
        .astype(jnp.bfloat16)
        .astype(jnp.float32)
    )
    part_up = (
        lax.dot_general(activation, incoming, contract_rows, preferred_element_type=jnp.float32)
        .astype(jnp.bfloat16)
        .astype(jnp.float32)
    )
    summed_down, summed_up = (
        lax.psum(part_down.astype(jnp.bfloat16), "peer").astype(jnp.float32),
        lax.psum(part_up.astype(jnp.bfloat16), "peer").astype(jnp.float32),
    )
    grad_down = (summed_down / peer_count).astype(jnp.bfloat16)
    grad_up = (summed_up / peer_count).astype(jnp.bfloat16)
    return (returned[None, None], grad_down[None], grad_up[None])


def solution(mesh):
    placed = (
        P("section", "peer", None, None, None),
        P("section", "peer", None, None, None),
        P("section", None, None),
        P("section", None, None),
        P("section", None),
        P("section", "peer", None),
        P("section", "peer"),
        P("section", "peer", None),
        P("section", "peer", None),
    )
    return jax.shard_map(
        on_device,
        mesh=mesh,
        in_specs=placed,
        out_specs=(
            P("section", "peer", None, None, None),
            P("section", None, None),
            P("section", None, None),
        ),
        check_vma=False,
    )
```

profile of v0, /device:TPU:1, one launch (start us, length us, event | category | flops | bytes accessed | tf_op | source)
XLA Modules:
  0.0 149.9 jit_solution(8055300727225198151)
XLA Ops:
  7.2 0.0 copy-start
  7.2 0.0 copy-start.2
  7.2 0.0 copy-start.3
  7.2 0.0 all-reduce.3.cloned.1.call-start
  7.2 0.8 convert_bitcast_fusion
  8.1 1.3 fusion.13
  9.3 0.1 rsqrt.13
  9.4 0.1 mul.98
  9.5 0.1 mul.99
  9.6 0.0 copy-done
  9.6 1.5 %fusion.3 = f32[24,144]{1,0:T(8,128)S(1)} fusion(bf16[1,144,5120]{2,1,0:T(8,128)(2,1)S(1)} %copy-done, f32[5120]{0:T(1024)} %bitcast.68, f32[3,8]{1,0:T(4,128)S(1)} %add_rsqrt_fusion, bf16[1,1,3,8,5120]{4,3,2,1,0:T(8,128)(2,1)} %param.9, bf16[3]{0:T(256)(128)(2,1)S(1)} %convert_bitcast_fusion), kind=kOutput, calls=%fused_computation.10 | convolution fusion | flops 36003840 | bytes 1754726 | tf_op jit(solution)/shard_map/dot_general | solution.py:46
  11.1 0.0 copy-done.2
  11.1 0.0 copy-done.3
  11.1 0.0 copy-start.1
  11.1 0.0 copy-start.4
  11.1 0.5 fusion.10
  11.7 1.7 %convolution_convert_fusion.2 = bf16[144,5120]{1,0:T(8,128)(2,1)} fusion(bf16[1,1,3,8,5120]{4,3,2,1,0:T(8,128)(2,1)S(1)} %copy-done.2, bf16[24]{0:T(256)(128)(2,1)S(1)} %mul.99, f32[24,144]{1,0:T(8,128)S(1)} %fusion.3), kind=kOutput, calls=%fused_computation.2 | convolution fusion | flops 36266880 | bytes 1734192 | tf_op jit(solution)/shard_map/dot_general | solution.py:77
  13.4 0.0 copy-done.1
  13.4 0.0 copy-done.4
  13.4 1.7 %convolution_convert_fusion.3 = bf16[144,5120]{1,0:T(8,128)(2,1)} fusion(bf16[24,144]{1,0:T(8,128)(2,1)S(1)} %fusion.10, f32[5120]{0:T(1024)S(1)} %bitcast.69, f32[24]{0:T(128)S(1)} %rsqrt.13, bf16[1,1,3,8,5120]{4,3,2,1,0:T(8,128)(2,1)S(1)} %copy-done.1, bf16[24]{0:T(256)(128)(2,1)S(1)} %mul.99), kind=kOutput, calls=%fused_computation.3 | convolution fusion | flops 36741120 | bytes 1747856 | tf_op jit(solution)/shard_map/dot_general | solution.py:72
  15.1 0.0 all-reduce.3.cloned.1.call-update
  15.1 0.0 copy-start.6
  15.1 0.0 copy-start.5
  15.2 0.4 multiply_reduce_fusion
  15.6 0.2 add_convert_fusion
  15.8 0.0 copy-start.7
  15.8 0.4 reshape.93
  16.2 0.0 copy-done.6
  16.2 0.0 copy-done.5
  16.2 0.3 convolution_convert_fusion.1
  16.6 0.1 copy.17
  16.7 22.9 %all_to_all.5 = bf16[4,8,5120]{2,1,0:T(8,128)(2,1)S(1)} all-to-all(bf16[4,8,5120]{2,1,0:T(8,128)(2,1)S(1)} %bitcast.63), channel_id=1, replica_groups=mesh['section'=8,'peer'=4] {'peer'}, dimensions={0} | all-to-all | bytes 655360 | tf_op jit(solution)/shard_map/all_to_all | solution.py:68
  39.6 3.4 %collective-permute-start = (bf16[4,8,5120]{2,1,0:T(8,128)(2,1)S(1)}, bf16[4,8,5120]{2,1,0:T(8,128)(2,1)S(1)}, u32[]{:S(2)}, u32[]{:S(2)}) collective-permute-start(bf16[4,8,5120]{2,1,0:T(8,128)(2,1)S(1)} %all_to_all.5), channel_id=1, source_target_pairs={{4,0},{8,4},{12,8},{16,12},{20,16},{24,20},{28,24},{0,28},{5,1},{9... | collective-permute-start | bytes 983048 | tf_op jit(solution)/shard_map/ppermute | solution.py:12
  43.6 5.6 %collective-permute-done = bf16[4,8,5120]{2,1,0:T(8,128)(2,1)S(1)} collective-permute-done((bf16[4,8,5120]{2,1,0:T(8,128)(2,1)S(1)}, bf16[4,8,5120]{2,1,0:T(8,128)(2,1)S(1)}, u32[]{:S(2)}, u32[]{:S(2)}) %collective-permute-start) | collective-permute-done | bytes 327712 | tf_op jit(solution)/shard_map/ppermute | solution.py:12
  49.2 0.3 copy.13
  49.4 0.0 copy-done.7
  49.4 0.4 convolution_convert_fusion
  49.8 0.8 copy.18
  50.6 88.4 %all-reduce.3.cloned.1.call-done = (bf16[144,5120]{1,0:T(8,128)(2,1)}, bf16[144,5120]{1,0:T(8,128)(2,1)}) async-done(((bf16[144,5120]{1,0:T(8,128)(2,1)}, bf16[144,5120]{1,0:T(8,128)(2,1)}), (bf16[144,5120]{1,0:T(8,128)(2,1)}, bf16[144,5120]{1,0:T(8,128)(2,1)})) %all-reduce.3.cloned.1.call-update) | async-done | bytes 2949136 | tf_op jit(solution)/shard_map/psum | solution.py:82
  139.0 4.0 %fusion = (bf16[1,144,5120]{2,1,0:T(8,128)(2,1)}, bf16[1,144,5120]{2,1,0:T(8,128)(2,1)}) fusion(bf16[144,5120]{1,0:T(8,128)(2,1)} %get-tuple-element.3, bf16[144,5120]{1,0:T(8,128)(2,1)} %get-tuple-element.4), kind=kLoop, calls=%fused_computation.7 | loop fusion | flops 4423680 | bytes 5898240 | tf_op jit(solution)/shard_map/broadcast_in_dim | solution.py:87
  (4 shorter events, 0.0 us)
Async XLA Ops:
  7.2 2.4 %copy-start = (bf16[1,144,5120]{2,1,0:T(8,128)(2,1)S(1)}, bf16[1,144,5120]{2,1,0:T(8,128)(2,1)}, u32[]{:S(2)}) copy-start(bf16[1,144,5120]{2,1,0:T(8,128)(2,1)} %param.11) | copy-start | bytes 4423684
  7.2 3.9 %copy-start.2 = (bf16[1,1,3,8,5120]{4,3,2,1,0:T(8,128)(2,1)S(1)}, bf16[1,1,3,8,5120]{4,3,2,1,0:T(8,128)(2,1)}, u32[]{:S(2)}) copy-start(bf16[1,1,3,8,5120]{4,3,2,1,0:T(8,128)(2,1)} %param.10) | copy-start | bytes 737284
  7.2 3.9 %copy-start.3 = (bf16[1,144,5120]{2,1,0:T(8,128)(2,1)S(1)}, bf16[1,144,5120]{2,1,0:T(8,128)(2,1)}, u32[]{:S(2)}) copy-start(bf16[1,144,5120]{2,1,0:T(8,128)(2,1)} %param.12) | copy-start | bytes 4423684
  7.2 131.8 %all-reduce.3.cloned.1.call-start = ((), (), s32[]{:S(2)}) async-start(), calls=%async_computation.1 | async-start | bytes 5898240 | tf_op jit(solution)/shard_map/psum | solution.py:82
  11.1 2.3 %copy-start.1 = (bf16[1,1,3,8,5120]{4,3,2,1,0:T(8,128)(2,1)S(1)}, bf16[1,1,3,8,5120]{4,3,2,1,0:T(8,128)(2,1)}, u32[]{:S(2)}) copy-start(bf16[1,1,3,8,5120]{4,3,2,1,0:T(8,128)(2,1)} %param.9) | copy-start | bytes 737284
  11.1 2.3 %copy-start.4 = (f32[1,5120]{1,0:T(1,128)S(1)}, f32[1,5120]{1,0:T(1,128)}, u32[]{:S(2)}) copy-start(f32[1,5120]{1,0:T(1,128)} %param.13) | copy-start | bytes 61444
  15.1 1.1 copy-start.6
  15.1 1.1 copy-start.5
  15.8 33.6 %copy-start.7 = (s32[1,1,3]{2,1,0:T(1,128)S(1)}, s32[1,1,3]{2,1,0:T(1,128)}, u32[]{:S(2)}) copy-start(s32[1,1,3]{2,1,0:T(1,128)} %param.14) | copy-start | bytes 40
  39.6 9.6 %collective-permute-start = (bf16[4,8,5120]{2,1,0:T(8,128)(2,1)S(1)}, bf16[4,8,5120]{2,1,0:T(8,128)(2,1)S(1)}, u32[]{:S(2)}, u32[]{:S(2)}) collective-permute-start(bf16[4,8,5120]{2,1,0:T(8,128)(2,1)S(1)} %all_to_all.5), channel_id=1, source_target_pairs={{4,0},{8,4},{12,8},{16,12},{20,16},{24,20},{28,24},{0,28},{5,1},{9... | collective-permute-start | bytes 983048 | tf_op jit(solution)/shard_map/ppermute | solution.py:12
Sparse Core Ops, SparseCore 0:
  15.3 123.7 all-reduce.2
where the time goes:
time: 151 us; the launch traced here: 150 us
  waiting for transfers between devices  94 us (62%)
  blocking collectives  22.9 us (15%)
  between operations  14.8 us (10%)
  matrix products  6.61 us (4%)
  other arithmetic  6.33 us (4%)
  starting transfers between devices  3.43 us (2%)
  local copies, waits for them, and re-layouts  1.82 us (1%)
    psum x1, waiting for transfers between devices, on_device(): lax.psum(part_down.astype(jnp.bfloat16), 'peer').astype(jnp.float32)  88.4 us
    all_to_all x1, blocking collectives, on_device(): lax.all_to_all(by_sender, 'peer', split_axis=0, concat_axis=0, tiled=True)  22.9 us
    ppermute x1, waiting for transfers between devices, passed_along(): return lax.ppermute(block, axis, route)  5.57 us
    broadcast_in_dim x1, other arithmetic, on_device(): return (returned[None, None], grad_down[None], grad_up[None])  4.01 us
    ppermute x1, starting transfers between devices, passed_along(): return lax.ppermute(block, axis, route)  3.39 us
  transfers between devices with their start and end apart: 2, of which 2 were waited for; matrix products, arithmetic and copies ran while one was open for 2% of the time, Pallas kernels for 0%

commit v1 on v0

--- a/solution.py
+++ b/solution.py
@@ -1,7 +1,15 @@
+import functools
+
 import jax
 import jax.numpy as jnp
 from jax import lax
+from jax.experimental import pallas as pl
+from jax.experimental.pallas import tpu as pltpu
 from jax.sharding import PartitionSpec as P
+
+MESH = pl.DeviceIdType.MESH
+LANES = 128
+WIDE = 256
 
 epsilon = 1e-05
 
@@ -87,6 +95,391 @@
     return (returned[None, None], grad_down[None], grad_up[None])
 
 
+def gather_kernel(
+    sections,
+    n,
+    parts,
+    stash,
+    back_in,
+    down,
+    up,
+    gain_ref,
+    sent_to,
+    sent_count,
+    recv_from,
+    back_live,
+    returned,
+    grad_down,
+    grad_up,
+    rows_all,
+    factors,
+    w_down,
+    w_up,
+    asked,
+    wanted,
+    picked,
+    local_sem,
+    right_sem,
+    left_sem,
+    recv_sem,
+    fac_right,
+    fac_left,
+    fac_recv,
+    want_sem,
+    back_send,
+    back_recv,
+):
+    section = lax.axis_index("section")
+    me = lax.axis_index("peer")
+    before = lax.rem(section + sections - 1, sections)
+    after = lax.rem(section + 1, sections)
+    rows, width = stash.shape
+    rank = down.shape[0]
+    part = width // parts
+    has_left, has_right = me > 0, me < n - 1
+
+    def cols(j):
+        return pl.ds(pl.multiple_of(j * part, part), part)
+
+    def along(origin, kind, j, step, own=False):
+        view = rows_all.at[origin, kind, :, cols(j)]
+        source = (stash, back_in)[kind].at[:, cols(j)] if own else view
+        return pltpu.make_async_remote_copy(
+            src_ref=source,
+            dst_ref=view,
+            send_sem=(right_sem if step > 0 else left_sem).at[origin, kind, j],
+            recv_sem=recv_sem.at[origin, kind, j],
+            device_id=(section, me + step),
+            device_id_type=MESH,
+        )
+
+    def factor_along(origin, step):
+        return pltpu.make_async_remote_copy(
+            src_ref=factors.at[origin],
+            dst_ref=factors.at[origin],
+            send_sem=(fac_right if step > 0 else fac_left).at[origin],
+            recv_sem=fac_recv.at[origin],
+            device_id=(section, me + step),
+            device_id_type=MESH,
+        )
+
+    def want_copy():
+        return pltpu.make_async_remote_copy(
+            src_ref=asked,
+            dst_ref=wanted,
+            send_sem=want_sem.at[0],
+            recv_sem=want_sem.at[1],
+            device_id=(after, me),
+            device_id_type=MESH,
+        )
+
+    def back_copy(j):
+        return pltpu.make_async_remote_copy(
+            src_ref=picked.at[:, cols(j)],
+            dst_ref=returned.at[:, cols(j)],
+            send_sem=back_send.at[j],
+            recv_sem=back_recv.at[j],
+            device_id=(before, me),
+            device_id_type=MESH,
+        )
+
+    loads = [
+        pltpu.make_async_copy(stash, rows_all.at[me, 0], local_sem.at[0]),
+        pltpu.make_async_copy(back_in, rows_all.at[me, 1], local_sem.at[1]),
+        pltpu.make_async_copy(down, w_down.at[pl.ds(0, rank)], local_sem.at[2]),
+        pltpu.make_async_copy(up, w_up.at[pl.ds(0, rank)], local_sem.at[3]),
+    ]
+    for load in loads:
+        load.start()
+
+    barrier = pltpu.get_barrier_semaphore()
+    for other in (before, after):
+        pl.semaphore_signal(barrier, inc=1, device_id=(other, me), device_id_type=MESH)
+
+    @pl.when(has_left)
+    def _():
+        pl.semaphore_signal(barrier, inc=1, device_id=(section, me - 1), device_id_type=MESH)
+
+    @pl.when(has_right)
+    def _():
+        pl.semaphore_signal(barrier, inc=1, device_id=(section, me + 1), device_id_type=MESH)
+
+    @pl.when(has_left & has_right)
+    def _():
+        pl.semaphore_wait(barrier, 4)
+
+    @pl.when(jnp.logical_not(has_left & has_right))
+    def _():
+        pl.semaphore_wait(barrier, 3)
+
+    for j in range(parts):
+        for kind in (0, 1):
+
+            @pl.when(has_right)
+            def _(j=j, kind=kind):
+                along(me, kind, j, 1, True).start()
+
+            @pl.when(has_left)
+            def _(j=j, kind=kind):
+                along(me, kind, j, -1, True).start()
+
+    slots = sent_to.shape[2]
+    micro = rows // slots
+    at_row = lax.broadcasted_iota(jnp.int32, (rows, LANES), 0)
+    at_lane = lax.broadcasted_iota(jnp.int32, (rows, LANES), 1)
+    lane_peer = jnp.zeros((rows, LANES), jnp.int32)
+    for a in range(1, n):
+        lane_peer += jnp.where(at_lane >= a * rows, 1, 0)
+    target = jnp.full((rows, LANES), -1, jnp.int32)
+    for k in range(slots):
+        here = (at_row >= k * micro) & (at_row < (k + 1) * micro)
+        target = jnp.where(here & (sent_count[0, 0] > k), sent_to[0, 0, k], target)
+    same = lax.rem(at_lane, micro) == lax.rem(at_row, micro)
+    asked[...] = jnp.where(same & (lane_peer == target), 1.0, 0.0)
+    want_copy().start()
+
+    w_down[pl.ds(rank, WIDE - rank), :] = jnp.zeros((WIDE - rank, width), jnp.bfloat16)
+    w_up[pl.ds(rank, WIDE - rank), :] = jnp.zeros((WIDE - rank, width), jnp.bfloat16)
+    for load in loads:
+        load.wait()
+
+    def square_part(j, total):
+        block = rows_all[me, 0, :, cols(j)].astype(jnp.float32)
+        return total + jnp.sum(block * block, axis=-1, keepdims=True)
+
+    squares = lax.fori_loop(0, parts, square_part, jnp.zeros((rows, 1), jnp.float32))
+    inverse = lax.rsqrt(squares / width + epsilon)
+    contract_last = (((1,), (1,)), ((), ()))
+
+    def project_part(j, carry):
+        pre, back = carry
+        block = rows_all[me, 0, :, cols(j)].astype(jnp.float32)
+        normed = (block * inverse * gain_ref[:, cols(j)]).astype(jnp.bfloat16)
+        pre = pre + lax.dot_general(
+            normed, w_down[:, cols(j)], contract_last, preferred_element_type=jnp.float32
+        )
+        back = back + lax.dot_general(
+            rows_all[me, 1, :, cols(j)],
+            w_up[:, cols(j)],
+            contract_last,
+            preferred_element_type=jnp.float32,
+        )
+        return pre, back
+
+    empty = jnp.zeros((rows, WIDE), jnp.float32)
+    preact, back_act = lax.fori_loop(0, parts, project_part, (empty, empty))
+    row_only = lax.broadcasted_iota(jnp.int32, (rows, 1), 0)
+    code_lane = lax.broadcasted_iota(jnp.int32, (8, LANES), 1) - me * rows
+    live = jnp.zeros((rows, 1), jnp.float32)
+    codes = jnp.zeros((8, LANES), jnp.float32)
+    for k in range(slots):
+        held = back_live[0, 0, k]
+        here = (row_only >= k * micro) & (row_only < (k + 1) * micro)
+        live = jnp.where(here, held.astype(jnp.float32), live)
+        here = (code_lane >= k * micro) & (code_lane < (k + 1) * micro)
+        codes = jnp.where(here, ((recv_from[0, 0, k] + 1) * held).astype(jnp.float32), codes)
+    sigmoid_pre = jax.nn.sigmoid(preact)
+    activation = preact * sigmoid_pre * live
+    back_pre = back_act * (sigmoid_pre * (1.0 + preact * (1.0 - sigmoid_pre))) * live
+    slope = jnp.sum(back_pre * preact, axis=-1, keepdims=True) * (inverse * inverse / width)
+    slope_high = slope.astype(jnp.bfloat16).astype(jnp.float32)
+    lane = lax.broadcasted_iota(jnp.int32, (rows, WIDE), 1)
+    second = jnp.where(lane == WIDE - 2, slope_high, activation)
+    second = jnp.where(lane == WIDE - 1, slope - slope_high, second)
+    zeros8 = jnp.zeros((8, LANES), jnp.float32)
+    tail = jnp.concatenate([codes, zeros8, zeros8, zeros8], axis=1)
+    body = jnp.concatenate([back_pre * inverse, second], axis=1)
+    factors[me] = jnp.concatenate([body, tail], axis=0).astype(jnp.bfloat16)
+
+    @pl.when(has_right)
+    def _():
+        factor_along(me, 1).start()
+
+    @pl.when(has_left)
+    def _():
+        factor_along(me, -1).start()
+
+    def arrivals(distance, j):
+        for step in (1, -1):
+            origin = me - step * distance
+            there = (origin >= 0) if step > 0 else (origin < n)
+            on = has_right if step > 0 else has_left
+
+            @pl.when(there)
+            def _(origin=origin, step=step, on=on):
+                for kind in (0, 1):
+                    along(origin, kind, j, step).wait_recv()
+
+                    @pl.when(on)
+                    def _(kind=kind):
+                        along(origin, kind, j, step).start()
+
+    def factor_arrivals(distance):
+        for step in (1, -1):
+            origin = me - step * distance
+            there = (origin >= 0) if step > 0 else (origin < n)
+            on = has_right if step > 0 else has_left
+
+            @pl.when(there)
+            def _(origin=origin, step=step, on=on):
+                factor_along(origin, step).wait_recv()
+
+                @pl.when(on)
+                def _():
+                    factor_along(origin, step).start()
+
+    for distance in range(1, n - 1):
+        for j in range(parts):
+            arrivals(distance, j)
+        factor_arrivals(distance)
+    factor_arrivals(n - 1)
+
+    want_copy().wait()
+    body_all = jnp.concatenate(
+        [factors[a, :, :].astype(jnp.float32)[:rows] for a in range(n)], axis=0
+    )
+    body_b = body_all.astype(jnp.bfloat16)
+    codes_all = factors[0, :, :].astype(jnp.float32)[rows : rows + 1, : n * rows]
+    for a in range(1, n):
+        codes_all += factors[a, :, :].astype(jnp.float32)[rows : rows + 1, : n * rows]
+    mine = (me + 1).astype(jnp.float32)
+    select = jnp.where(codes_all == mine, wanted[...][:, : n * rows], 0.0).astype(jnp.bfloat16)
+    chosen = jnp.dot(select, body_b, preferred_element_type=jnp.float32)
+    chosen_back = chosen[:, :WIDE].astype(jnp.bfloat16)
+    chosen_slope = jnp.sum(
+        jnp.where(lane >= WIDE - 2, chosen[:, WIDE:], 0.0), axis=-1, keepdims=True
+    )
+    weights_t = jnp.transpose(body_all)
+    down_t = weights_t[:rank].astype(jnp.bfloat16)
+    up_t = weights_t[WIDE : WIDE + rank].astype(jnp.bfloat16)
+
+    def finish(j, carry):
+        arrivals(n - 1, j)
+        gain = gain_ref[:, cols(j)]
+
+        def whole(kind):
+            blocks = [rows_all[a, kind, :, cols(j)].astype(jnp.float32) for a in range(n)]
+            return jnp.concatenate(blocks, axis=0).astype(jnp.bfloat16)
+
+        stash_all, back_all = whole(0), whole(1)
+        through = jnp.dot(chosen_back, w_down[:, cols(j)], preferred_element_type=jnp.float32)
+        chosen_in = jnp.dot(select, back_all, preferred_element_type=jnp.float32)
+        chosen_stash = jnp.dot(select, stash_all, preferred_element_type=jnp.float32)
+        out = chosen_in + through * gain - chosen_slope * chosen_stash
+        picked[:, cols(j)] = out.astype(jnp.bfloat16)
+        back_copy(j).start()
+        sum_down = jnp.dot(down_t, stash_all, preferred_element_type=jnp.float32)
+        grad_down[:, cols(j)] = (sum_down * (gain / n)).astype(jnp.bfloat16)
+        sum_up = jnp.dot(up_t, back_all, preferred_element_type=jnp.float32)
+        grad_up[:, cols(j)] = (sum_up / n).astype(jnp.bfloat16)
+        return carry
+
+    lax.fori_loop(0, parts, finish, 0)
+
+    def drain(j, carry):
+        back_copy(j).wait()
+        for kind in (0, 1):
+
+            @pl.when(has_right)
+            def _(kind=kind):
+                along(me, kind, j, 1, True).wait_send()
+
+            @pl.when(has_left)
+            def _(kind=kind):
+                along(me, kind, j, -1, True).wait_send()
+
+        for distance in range(1, n):
+            for step in (1, -1):
+                origin = me - step * distance
+                there = (origin >= 0) if step > 0 else (origin < n)
+                on = has_right if step > 0 else has_left
+
+                @pl.when(there & on)
+                def _(origin=origin, step=step):
+                    for kind in (0, 1):
+                        along(origin, kind, j, step).wait_send()
+
+        return carry
+
+    lax.fori_loop(0, parts, drain, 0)
+
+    for distance in range(n):
+        for step in (1, -1):
+            if distance == 0 or distance < n - 1:
+                origin = me - step * distance
+                there = (origin >= 0) if step > 0 else (origin < n)
+                on = has_right if step > 0 else has_left
+
+                @pl.when(there & on)
+                def _(origin=origin, step=step):
+                    factor_along(origin, step).wait_send()
+
+
+def gathered(stash, back_in, down_proj, up_proj, gain, sent_to, sent_count, recv_from, back_live):
+    sections, n = lax.axis_size("section"), lax.axis_size("peer")
+    slots, micro, width = stash.shape[2:]
+    rows = slots * micro
+    rank = down_proj.shape[1]
+    parts = 4
+    hbm = pl.BlockSpec(memory_space=pl.ANY)
+    vmem = pl.BlockSpec(memory_space=pltpu.VMEM)
+    smem = pl.BlockSpec(memory_space=pltpu.SMEM)
+    dma = pltpu.SemaphoreType.DMA
+    returned, grad_down, grad_up = pl.pallas_call(
+        functools.partial(gather_kernel, sections, n, parts),
+        out_shape=(
+            jax.ShapeDtypeStruct((rows, width), jnp.bfloat16),
+            jax.ShapeDtypeStruct((rank, width), jnp.bfloat16),
+            jax.ShapeDtypeStruct((rank, width), jnp.bfloat16),
+        ),
+        in_specs=[hbm, hbm, hbm, hbm, vmem, smem, smem, smem, smem],
+        out_specs=(vmem, vmem, vmem),
+        scratch_shapes=[
+            pltpu.VMEM((n, 2, rows, width), jnp.bfloat16),
+            pltpu.VMEM((n, rows + 8, 2 * WIDE), jnp.bfloat16),
+            pltpu.VMEM((WIDE, width), jnp.bfloat16),
+            pltpu.VMEM((WIDE, width), jnp.bfloat16),
+            pltpu.VMEM((rows, LANES), jnp.float32),
+            pltpu.VMEM((rows, LANES), jnp.float32),
+            pltpu.VMEM((rows, width), jnp.bfloat16),
+            dma((4,)),
+            dma((n, 2, parts)),
+            dma((n, 2, parts)),
+            dma((n, 2, parts)),
+            dma((n,)),
+            dma((n,)),
+            dma((n,)),
+            dma((2,)),
+            dma((parts,)),
+            dma((parts,)),
+        ],
+        compiler_params=pltpu.CompilerParams(
+            collective_id=0, has_side_effects=True, vmem_limit_bytes=40 * 1024 * 1024
+        ),
+        cost_estimate=pl.CostEstimate(
+            flops=10 * n * rows * rank * width, bytes_accessed=16 * rank * width, transcendentals=0
+        ),
+    )(
+        stash.reshape(rows, width),
+        back_in.reshape(rows, width),
+        down_proj[0],
+        up_proj[0],
+        gain,
+        sent_to,
+        sent_count,
+        recv_from,
+        back_live,
+    )
+    return returned.reshape(stash.shape), grad_down[None], grad_up[None]
+
+
+def by_size(stash, *rest):
+    n, sections = lax.axis_size("peer"), lax.axis_size("section")
+    rows = stash.shape[2] * stash.shape[3]
+    few = n * rows <= LANES and n > 2 and sections > 2
+    return (gathered if few else on_device)(stash, *rest)
+
+
 def solution(mesh):
     placed = (
         P("section", "peer", None, None, None),
@@ -100,7 +493,7 @@
         P("section", "peer", None),
     )
     return jax.shard_map(
-        on_device,
+        by_size,
         mesh=mesh,
         in_specs=placed,
         out_specs=(

time: 151 us -> 59.6 us (0.39)
  waiting for transfers between devices: 94 us -> 0 us
  Pallas kernels: 0 us -> 47.7 us
  blocking collectives: 22.9 us -> 0 us
  between operations: 14.8 us -> 1.3 us
  local copies, waits for them, and re-layouts: 1.82 us -> 10.2 us
  matrix products: 6.61 us -> 0 us
  other arithmetic: 6.33 us -> 0 us
  starting transfers between devices: 3.43 us -> 0 us
    psum x1 -> x0, waiting for transfers between devices: 88.4 us -> none  [on_device(): lax.psum(part_down.astype(jnp.bfloat16), 'peer').astype(jnp.float32)]
    pallas_call x0 -> x1, Pallas kernels: none -> 47.7 us  [gathered(): pl.pallas_call(functools.partial(gather_kernel, sections, n, parts), out_...]
    all_to_all x1 -> x0, blocking collectives: 22.9 us -> none  [on_device(): lax.all_to_all(by_sender, 'peer', split_axis=0, concat_axis=0, tiled=True)]
    unnamed x19, local copies, waits for them, and re-layouts: 1.22 us -> 10.2 us
    dot_general x7 -> x0, matrix products: 6.61 us -> none  [the longest x1 1.72 us: on_device(): lax.dot_general(back_pre, normed, contract_rows, preferred_element_type=j...]
    ppermute x1 -> x0, waiting for transfers between devices: 5.57 us -> none  [passed_along(): return lax.ppermute(block, axis, route)]
    broadcast_in_dim x1 -> x0, other arithmetic: 4.01 us -> none  [on_device(): return (returned[None, None], grad_down[None], grad_up[None])]
    ppermute x1 -> x0, starting transfers between devices: 3.39 us -> none  [passed_along(): return lax.ppermute(block, axis, route)]
  transfers between devices with their start and end apart: 2 -> 0, of which waited for: 2 -> 0; matrix products, arithmetic and copies ran while one was open for 2% -> 0% of each run, Pallas kernels for 0% -> 0%
where the time goes in v1:
time: 59.6 us; the launch traced here: 59.2 us
  Pallas kernels  47.7 us (80%)
  local copies, waits for them, and re-layouts  10.2 us (17%)
  between operations  1.3 us (2%)
    pallas_call x1, Pallas kernels, gathered(): pl.pallas_call(functools.partial(gather_kernel, sections, n, parts), out_...  47.7 us
    unnamed x19, local copies, waits for them, and re-layouts  10.2 us

profile of v1, /device:TPU:1, one launch (start us, length us, event | category | flops | bytes accessed | tf_op | source)
XLA Modules:
  0.0 59.2 jit_solution(754658715102247911)
XLA Ops:
  1.3 0.0 copy-start
  1.3 1.4 %copy-done = bf16[1,144,5120]{2,1,0:T(8,128)(2,1)S(1)} copy-done((bf16[1,144,5120]{2,1,0:T(8,128)(2,1)S(1)}, bf16[1,144,5120]{2,1,0:T(8,128)(2,1)}, u32[]{:S(2)}) %copy-start) | copy-done | bytes 1474584
  2.7 0.0 copy-start.1
  2.7 1.4 %copy-done.1 = bf16[1,144,5120]{2,1,0:T(8,128)(2,1)S(1)} copy-done((bf16[1,144,5120]{2,1,0:T(8,128)(2,1)S(1)}, bf16[1,144,5120]{2,1,0:T(8,128)(2,1)}, u32[]{:S(2)}) %copy-start.1) | copy-done | bytes 1474584
  4.0 0.0 copy-start.2
  4.0 0.9 %copy-done.2 = bf16[1,1,3,8,5120]{4,3,2,1,0:T(8,128)(2,1)S(1)} copy-done((bf16[1,1,3,8,5120]{4,3,2,1,0:T(8,128)(2,1)S(1)}, bf16[1,1,3,8,5120]{4,3,2,1,0:T(8,128)(2,1)}, u32[]{:S(2)}) %copy-start.2) | copy-done | bytes 245784
  5.0 0.0 copy-start.3
  5.0 0.9 %copy-done.3 = bf16[1,1,3,8,5120]{4,3,2,1,0:T(8,128)(2,1)S(1)} copy-done((bf16[1,1,3,8,5120]{4,3,2,1,0:T(8,128)(2,1)S(1)}, bf16[1,1,3,8,5120]{4,3,2,1,0:T(8,128)(2,1)}, u32[]{:S(2)}) %copy-start.3) | copy-done | bytes 245784
  5.9 0.0 copy-start.4
  5.9 0.7 %copy-done.4 = f32[1,5120]{1,0:T(1,128)S(1)} copy-done((f32[1,5120]{1,0:T(1,128)S(1)}, f32[1,5120]{1,0:T(1,128)}, u32[]{:S(2)}) %copy-start.4) | copy-done | bytes 20504
  6.6 0.0 copy-start.5
  6.6 0.7 %copy-done.5 = s32[1,1,3]{2,1,0:T(1,128)S(1)} copy-done((s32[1,1,3]{2,1,0:T(1,128)S(1)}, s32[1,1,3]{2,1,0:T(1,128)}, u32[]{:S(2)}) %copy-start.5) | copy-done | bytes 36
  7.3 0.0 copy-start.6
  7.3 0.7 %copy-done.6 = s32[1,1,3]{2,1,0:T(1,128)S(1)} copy-done((s32[1,1,3]{2,1,0:T(1,128)S(1)}, s32[1,1,3]{2,1,0:T(1,128)}, u32[]{:S(2)}) %copy-start.6) | copy-done | bytes 36
  8.0 0.0 copy-start.7
  8.0 0.7 %copy-done.7 = s32[1,1,3]{2,1,0:T(1,128)S(1)} copy-done((s32[1,1,3]{2,1,0:T(1,128)S(1)}, s32[1,1,3]{2,1,0:T(1,128)}, u32[]{:S(2)}) %copy-start.7) | copy-done | bytes 36
  8.6 47.7 %shard_map.112 = (bf16[24,5120]{1,0:T(8,128)(2,1)S(1)}, bf16[144,5120]{1,0:T(8,128)(2,1)S(1)}, bf16[144,5120]{1,0:T(8,128)(2,1)S(1)}) custom-call(bf16[24,5120]{1,0:T(8,128)(2,1)S(1)} %bitcast.11, bf16[24,5120]{1,0:T(8,128)(2,1)S(1)} %bitcast.12, bf16[144,5120]{1,0:T(8,128)(2,1)S(1)} %bitcast.7, bf16[144,5120]{1,0:T(8,128)(2,1)S(1)} %bitcast.8, ...), custom_call_target="tpu_custom_call" | custom-call | flops 707788800 | bytes 11796480 | tf_op jit(solution)/shard_map/pallas_call | solution.py:428
  56.3 0.7 %copy.16 = bf16[1,1,3,8,5120]{4,3,2,1,0:T(8,128)(2,1)} copy(bf16[1,1,3,8,5120]{4,3,2,1,0:T(8,128)(2,1)S(1)} %bitcast.13) | data formatting | bytes 491520
  57.0 1.1 %copy.17 = bf16[1,144,5120]{2,1,0:T(8,128)(2,1)} copy(bf16[1,144,5120]{2,1,0:T(8,128)(2,1)S(1)} %bitcast.10) | data formatting | bytes 2949120
  58.1 1.1 %copy.18 = bf16[1,144,5120]{2,1,0:T(8,128)(2,1)} copy(bf16[1,144,5120]{2,1,0:T(8,128)(2,1)S(1)} %bitcast.9) | data formatting | bytes 2949120
Async XLA Ops:
  1.3 1.4 %copy-start = (bf16[1,144,5120]{2,1,0:T(8,128)(2,1)S(1)}, bf16[1,144,5120]{2,1,0:T(8,128)(2,1)}, u32[]{:S(2)}) copy-start(bf16[1,144,5120]{2,1,0:T(8,128)(2,1)} %param.11) | copy-start | bytes 4423684
  2.7 1.4 %copy-start.1 = (bf16[1,144,5120]{2,1,0:T(8,128)(2,1)S(1)}, bf16[1,144,5120]{2,1,0:T(8,128)(2,1)}, u32[]{:S(2)}) copy-start(bf16[1,144,5120]{2,1,0:T(8,128)(2,1)} %param.12) | copy-start | bytes 4423684
  4.0 0.9 %copy-start.2 = (bf16[1,1,3,8,5120]{4,3,2,1,0:T(8,128)(2,1)S(1)}, bf16[1,1,3,8,5120]{4,3,2,1,0:T(8,128)(2,1)}, u32[]{:S(2)}) copy-start(bf16[1,1,3,8,5120]{4,3,2,1,0:T(8,128)(2,1)} %param.9) | copy-start | bytes 737284
  5.0 0.9 %copy-start.3 = (bf16[1,1,3,8,5120]{4,3,2,1,0:T(8,128)(2,1)S(1)}, bf16[1,1,3,8,5120]{4,3,2,1,0:T(8,128)(2,1)}, u32[]{:S(2)}) copy-start(bf16[1,1,3,8,5120]{4,3,2,1,0:T(8,128)(2,1)} %param.10) | copy-start | bytes 737284
  5.9 0.7 %copy-start.4 = (f32[1,5120]{1,0:T(1,128)S(1)}, f32[1,5120]{1,0:T(1,128)}, u32[]{:S(2)}) copy-start(f32[1,5120]{1,0:T(1,128)} %gain_ref.1) | copy-start | bytes 61444
  6.6 0.7 %copy-start.5 = (s32[1,1,3]{2,1,0:T(1,128)S(1)}, s32[1,1,3]{2,1,0:T(1,128)}, u32[]{:S(2)}) copy-start(s32[1,1,3]{2,1,0:T(1,128)} %sent_to.1) | copy-start | bytes 40
  7.3 0.7 %copy-start.6 = (s32[1,1,3]{2,1,0:T(1,128)S(1)}, s32[1,1,3]{2,1,0:T(1,128)}, u32[]{:S(2)}) copy-start(s32[1,1,3]{2,1,0:T(1,128)} %recv_from.1) | copy-start | bytes 40
  8.0 0.7 %copy-start.7 = (s32[1,1,3]{2,1,0:T(1,128)S(1)}, s32[1,1,3]{2,1,0:T(1,128)}, u32[]{:S(2)}) copy-start(s32[1,1,3]{2,1,0:T(1,128)} %back_live.1) | copy-start | bytes 40

commit v2 on v1

--- a/solution.py
+++ b/solution.py
@@ -103,14 +103,14 @@
     back_in,
     down,
     up,
-    gain_ref,
-    sent_to,
-    sent_count,
-    recv_from,
-    back_live,
+    gain_in,
+    sent_to_in,
+    sent_count_in,
+    recv_from_in,
+    back_live_in,
     returned,
-    grad_down,
-    grad_up,
+    grad_down_out,
+    grad_up_out,
     rows_all,
     factors,
     w_down,
@@ -118,6 +118,13 @@
     asked,
     wanted,
     picked,
+    grad_down,
+    grad_up,
+    gain_ref,
+    sent_to,
+    sent_count,
+    recv_from,
+    back_live,
     local_sem,
     right_sem,
     left_sem,
@@ -128,6 +135,7 @@
     want_sem,
     back_send,
     back_recv,
+    out_sem,
 ):
     section = lax.axis_index("section")
     me = lax.axis_index("peer")
@@ -183,13 +191,30 @@
             device_id_type=MESH,
         )
 
+    small = [
+        pltpu.make_async_copy(sent_to_in, sent_to, local_sem.at[5]),
+        pltpu.make_async_copy(sent_count_in, sent_count, local_sem.at[6]),
+        pltpu.make_async_copy(recv_from_in, recv_from, local_sem.at[7]),
+        pltpu.make_async_copy(back_live_in, back_live, local_sem.at[8]),
+    ]
+    def stores(j):
+        return (
+            pltpu.make_async_copy(
+                grad_down.at[:, cols(j)], grad_down_out.at[:, cols(j)], out_sem.at[0, j]
+            ),
+            pltpu.make_async_copy(
+                grad_up.at[:, cols(j)], grad_up_out.at[:, cols(j)], out_sem.at[1, j]
+            ),
+        )
+
     loads = [
         pltpu.make_async_copy(stash, rows_all.at[me, 0], local_sem.at[0]),
         pltpu.make_async_copy(back_in, rows_all.at[me, 1], local_sem.at[1]),
         pltpu.make_async_copy(down, w_down.at[pl.ds(0, rank)], local_sem.at[2]),
         pltpu.make_async_copy(up, w_up.at[pl.ds(0, rank)], local_sem.at[3]),
+        pltpu.make_async_copy(gain_in, gain_ref, local_sem.at[4]),
     ]
-    for load in loads:
+    for load in small + loads:
         load.start()
 
     barrier = pltpu.get_barrier_semaphore()
@@ -223,6 +248,8 @@
             def _(j=j, kind=kind):
                 along(me, kind, j, -1, True).start()
 
+    for load in small:
+        load.wait()
     slots = sent_to.shape[2]
     micro = rows // slots
     at_row = lax.broadcasted_iota(jnp.int32, (rows, LANES), 0)
@@ -328,11 +355,12 @@
                 def _():
                     factor_along(origin, step).start()
 
-    for distance in range(1, n - 1):
-        for j in range(parts):
-            arrivals(distance, j)
+    for distance in range(1, n):
+        arrivals(distance, 0)
         factor_arrivals(distance)
-    factor_arrivals(n - 1)
+        if distance < n - 1:
+            for j in range(1, parts):
+                arrivals(distance, j)
 
     want_copy().wait()
     body_all = jnp.concatenate(
@@ -354,7 +382,10 @@
     up_t = weights_t[WIDE : WIDE + rank].astype(jnp.bfloat16)
 
     def finish(j, carry):
-        arrivals(n - 1, j)
+        @pl.when(j > 0)
+        def _():
+            arrivals(n - 1, j)
+
         gain = gain_ref[:, cols(j)]
 
         def whole(kind):
@@ -372,12 +403,16 @@
         grad_down[:, cols(j)] = (sum_down * (gain / n)).astype(jnp.bfloat16)
         sum_up = jnp.dot(up_t, back_all, preferred_element_type=jnp.float32)
         grad_up[:, cols(j)] = (sum_up / n).astype(jnp.bfloat16)
+        for store in stores(j):
+            store.start()
         return carry
 
     lax.fori_loop(0, parts, finish, 0)
 
     def drain(j, carry):
         back_copy(j).wait()
+        for store in stores(j):
+            store.wait()
         for kind in (0, 1):
 
             @pl.when(has_right)
@@ -421,9 +456,7 @@
     rows = slots * micro
     rank = down_proj.shape[1]
     parts = 4
-    hbm = pl.BlockSpec(memory_space=pl.ANY)
-    vmem = pl.BlockSpec(memory_space=pltpu.VMEM)
-    smem = pl.BlockSpec(memory_space=pltpu.SMEM)
+    hbm = pl.BlockSpec(memory_space=pltpu.HBM)
     dma = pltpu.SemaphoreType.DMA
     returned, grad_down, grad_up = pl.pallas_call(
         functools.partial(gather_kernel, sections, n, parts),
@@ -432,8 +465,8 @@
             jax.ShapeDtypeStruct((rank, width), jnp.bfloat16),
             jax.ShapeDtypeStruct((rank, width), jnp.bfloat16),
         ),
-        in_specs=[hbm, hbm, hbm, hbm, vmem, smem, smem, smem, smem],
-        out_specs=(vmem, vmem, vmem),
+        in_specs=[hbm] * 9,
+        out_specs=(hbm, hbm, hbm),
         scratch_shapes=[
             pltpu.VMEM((n, 2, rows, width), jnp.bfloat16),
             pltpu.VMEM((n, rows + 8, 2 * WIDE), jnp.bfloat16),
@@ -442,7 +475,14 @@
             pltpu.VMEM((rows, LANES), jnp.float32),
             pltpu.VMEM((rows, LANES), jnp.float32),
             pltpu.VMEM((rows, width), jnp.bfloat16),
-            dma((4,)),
+            pltpu.VMEM((rank, width), jnp.bfloat16),
+            pltpu.VMEM((rank, width), jnp.bfloat16),
+            pltpu.VMEM((1, width), jnp.float32),
+            pltpu.SMEM(sent_to.shape, jnp.int32),
+            pltpu.SMEM(sent_count.shape, jnp.int32),
+            pltpu.SMEM(recv_from.shape, jnp.int32),
+            pltpu.SMEM(back_live.shape, jnp.int32),
+            dma((9,)),
             dma((n, 2, parts)),
             dma((n, 2, parts)),
             dma((n, 2, parts)),
@@ -452,9 +492,10 @@
             dma((2,)),
             dma((parts,)),
             dma((parts,)),
+            dma((2, parts)),
         ],
         compiler_params=pltpu.CompilerParams(
-            collective_id=0, has_side_effects=True, vmem_limit_bytes=40 * 1024 * 1024
+            collective_id=0, has_side_effects=True, vmem_limit_bytes=60 * 1024 * 1024
         ),
         cost_estimate=pl.CostEstimate(
             flops=10 * n * rows * rank * width, bytes_accessed=16 * rank * width, transcendentals=0

time: 59.6 us -> 51.1 us (0.86)
  local copies, waits for them, and re-layouts: 10.2 us -> 5.46 us
  Pallas kernels: 47.7 us -> 44.1 us
    unnamed x19 -> x5, local copies, waits for them, and re-layouts: 10.2 us -> 5.46 us
    pallas_call x1, Pallas kernels: 47.7 us -> 44.1 us  [gathered(): pl.pallas_call(functools.partial(gather_kernel, sections, n, parts), out_...]
where the time goes in v2:
time: 51.1 us; the launch traced here: 50.9 us
  Pallas kernels  44.1 us (86%)
  local copies, waits for them, and re-layouts  5.46 us (11%)
  between operations  1.29 us (3%)
    pallas_call x1, Pallas kernels, gathered(): pl.pallas_call(functools.partial(gather_kernel, sections, n, parts), out_...  44.1 us
    unnamed x5, local copies, waits for them, and re-layouts  5.46 us

profile of v2, /device:TPU:1, one launch (start us, length us, event | category | flops | bytes accessed | tf_op | source)
XLA Modules:
  0.0 50.9 jit_solution(166843496385607705)
XLA Ops:
  1.3 44.1 %shard_map.112 = (bf16[24,5120]{1,0:T(8,128)(2,1)}, bf16[144,5120]{1,0:T(8,128)(2,1)}, bf16[144,5120]{1,0:T(8,128)(2,1)}) custom-call(bf16[24,5120]{1,0:T(8,128)(2,1)} %bitcast.11, bf16[24,5120]{1,0:T(8,128)(2,1)} %bitcast.12, bf16[144,5120]{1,0:T(8,128)(2,1)} %bitcast.7, bf16[144,5120]{1,0:T(8,128)(2,1)} %bitcast.8, f32[1,5120]{1,0:T(1,128)} %gain_in.1, ...), custom_call_target="tpu_custom_call" | custom-call | flops 707788800 | bytes 11796480 | tf_op jit(solution)/shard_map/pallas_call | solution.py:461
  45.4 1.7 %copy.16 = bf16[1,1,3,8,5120]{4,3,2,1,0:T(8,128)(2,1)} copy(bf16[1,1,3,8,5120]{4,3,2,1,0:T(8,128)(2,1)} %bitcast.13) | data formatting | bytes 491520
  47.1 0.0 copy-start
  47.1 2.7 %copy.17 = bf16[1,144,5120]{2,1,0:T(8,128)(2,1)} copy(bf16[1,144,5120]{2,1,0:T(8,128)(2,1)} %bitcast.10) | data formatting | bytes 2949120
  49.8 0.0 copy-done
  49.8 1.1 %copy.18 = bf16[1,144,5120]{2,1,0:T(8,128)(2,1)} copy(bf16[1,144,5120]{2,1,0:T(8,128)(2,1)S(1)} %bitcast.9) | data formatting | bytes 2949120
Async XLA Ops:
  47.1 2.7 %copy-start = (bf16[144,5120]{1,0:T(8,128)(2,1)S(1)}, bf16[144,5120]{1,0:T(8,128)(2,1)}, u32[]{:S(2)}) copy-start(bf16[144,5120]{1,0:T(8,128)(2,1)} %get-tuple-element.8) | copy-start | bytes 4423684

commit v3 on v2

--- a/solution.py
+++ b/solution.py
@@ -296,27 +296,26 @@
     empty = jnp.zeros((rows, WIDE), jnp.float32)
     preact, back_act = lax.fori_loop(0, parts, project_part, (empty, empty))
     row_only = lax.broadcasted_iota(jnp.int32, (rows, 1), 0)
-    code_lane = lax.broadcasted_iota(jnp.int32, (8, LANES), 1) - me * rows
     live = jnp.zeros((rows, 1), jnp.float32)
-    codes = jnp.zeros((8, LANES), jnp.float32)
+    code = jnp.zeros((rows, 1), jnp.float32)
     for k in range(slots):
         held = back_live[0, 0, k]
         here = (row_only >= k * micro) & (row_only < (k + 1) * micro)
         live = jnp.where(here, held.astype(jnp.float32), live)
-        here = (code_lane >= k * micro) & (code_lane < (k + 1) * micro)
-        codes = jnp.where(here, ((recv_from[0, 0, k] + 1) * held).astype(jnp.float32), codes)
+        code = jnp.where(here, ((recv_from[0, 0, k] + 1) * held).astype(jnp.float32), code)
     sigmoid_pre = jax.nn.sigmoid(preact)
     activation = preact * sigmoid_pre * live
     back_pre = back_act * (sigmoid_pre * (1.0 + preact * (1.0 - sigmoid_pre))) * live
     slope = jnp.sum(back_pre * preact, axis=-1, keepdims=True) * (inverse * inverse / width)
     slope_high = slope.astype(jnp.bfloat16).astype(jnp.float32)
-    lane = lax.broadcasted_iota(jnp.int32, (rows, WIDE), 1)
-    second = jnp.where(lane == WIDE - 2, slope_high, activation)
-    second = jnp.where(lane == WIDE - 1, slope - slope_high, second)
-    zeros8 = jnp.zeros((8, LANES), jnp.float32)
-    tail = jnp.concatenate([codes, zeros8, zeros8, zeros8], axis=1)
-    body = jnp.concatenate([back_pre * inverse, second], axis=1)
-    factors[me] = jnp.concatenate([body, tail], axis=0).astype(jnp.bfloat16)
+    packed = factors.shape[2]
+    extra = jnp.zeros((rows, packed - WIDE), jnp.float32)
+    lane = lax.broadcasted_iota(jnp.int32, (rows, packed), 1)
+    body = jnp.concatenate([back_pre * inverse, extra], axis=1)
+    body += pltpu.roll(jnp.concatenate([activation, extra], axis=1), rank, 1)
+    for at, value in enumerate((slope_high, slope - slope_high, code)):
+        body = jnp.where(lane == 2 * rank + at, value, body)
+    factors[me] = body.astype(jnp.bfloat16)
 
     @pl.when(has_right)
     def _():
@@ -363,23 +362,19 @@
                 arrivals(distance, j)
 
     want_copy().wait()
-    body_all = jnp.concatenate(
-        [factors[a, :, :].astype(jnp.float32)[:rows] for a in range(n)], axis=0
-    )
-    body_b = body_all.astype(jnp.bfloat16)
-    codes_all = factors[0, :, :].astype(jnp.float32)[rows : rows + 1, : n * rows]
-    for a in range(1, n):
-        codes_all += factors[a, :, :].astype(jnp.float32)[rows : rows + 1, : n * rows]
+    body_all = jnp.concatenate([factors[a].astype(jnp.float32) for a in range(n)], axis=0)
+    body_t = jnp.transpose(body_all)
     mine = (me + 1).astype(jnp.float32)
-    select = jnp.where(codes_all == mine, wanted[...][:, : n * rows], 0.0).astype(jnp.bfloat16)
-    chosen = jnp.dot(select, body_b, preferred_element_type=jnp.float32)
+    codes_all = body_t[2 * rank + 2 : 2 * rank + 3]
+    select = jnp.where(codes_all == mine, wanted[...][:, : n * rows], 0.0)
+    chosen = jnp.dot(
+        select.astype(jnp.bfloat16), body_all.astype(jnp.bfloat16), preferred_element_type=jnp.float32
+    )
     chosen_back = chosen[:, :WIDE].astype(jnp.bfloat16)
-    chosen_slope = jnp.sum(
-        jnp.where(lane >= WIDE - 2, chosen[:, WIDE:], 0.0), axis=-1, keepdims=True
-    )
-    weights_t = jnp.transpose(body_all)
-    down_t = weights_t[:rank].astype(jnp.bfloat16)
-    up_t = weights_t[WIDE : WIDE + rank].astype(jnp.bfloat16)
+    slope_lane = (lane == 2 * rank) | (lane == 2 * rank + 1)
+    chosen_slope = jnp.sum(jnp.where(slope_lane, chosen, 0.0), axis=-1, keepdims=True)
+    down_pick = jnp.concatenate([select, body_t[:rank]], axis=0).astype(jnp.bfloat16)
+    up_pick = jnp.concatenate([select, body_t[rank : 2 * rank]], axis=0).astype(jnp.bfloat16)
 
     def finish(j, carry):
         @pl.when(j > 0)
@@ -394,15 +389,13 @@
 
         stash_all, back_all = whole(0), whole(1)
         through = jnp.dot(chosen_back, w_down[:, cols(j)], preferred_element_type=jnp.float32)
-        chosen_in = jnp.dot(select, back_all, preferred_element_type=jnp.float32)
-        chosen_stash = jnp.dot(select, stash_all, preferred_element_type=jnp.float32)
-        out = chosen_in + through * gain - chosen_slope * chosen_stash
+        from_stash = jnp.dot(down_pick, stash_all, preferred_element_type=jnp.float32)
+        from_back = jnp.dot(up_pick, back_all, preferred_element_type=jnp.float32)
+        out = from_back[:rows] + through * gain - chosen_slope * from_stash[:rows]
         picked[:, cols(j)] = out.astype(jnp.bfloat16)
         back_copy(j).start()
-        sum_down = jnp.dot(down_t, stash_all, preferred_element_type=jnp.float32)
-        grad_down[:, cols(j)] = (sum_down * (gain / n)).astype(jnp.bfloat16)
-        sum_up = jnp.dot(up_t, back_all, preferred_element_type=jnp.float32)
-        grad_up[:, cols(j)] = (sum_up / n).astype(jnp.bfloat16)
+        grad_down[:, cols(j)] = (from_stash[rows:] * (gain / n)).astype(jnp.bfloat16)
+        grad_up[:, cols(j)] = (from_back[rows:] / n).astype(jnp.bfloat16)
         for store in stores(j):
             store.start()
         return carry
@@ -450,15 +443,31 @@
                     factor_along(origin, step).wait_send()
 
 
+def place_kernel(*refs):
+    copies = []
+    for i in range(3):
+        source, target, sem = refs[i], refs[3 + i], refs[6]
+        height = source.shape[0]
+        pieces = 3 if height % 48 == 0 else 1
+        for piece in range(pieces):
+            span = pl.ds(piece * (height // pieces), height // pieces)
+            copies.append(pltpu.make_async_copy(source.at[span], target.at[span], sem.at[i, piece]))
+    for copy in copies:
+        copy.start()
+    for copy in copies:
+        copy.wait()
+
+
 def gathered(stash, back_in, down_proj, up_proj, gain, sent_to, sent_count, recv_from, back_live):
     sections, n = lax.axis_size("section"), lax.axis_size("peer")
     slots, micro, width = stash.shape[2:]
     rows = slots * micro
     rank = down_proj.shape[1]
     parts = 4
+    packed = -(-(2 * rank + 3) // LANES) * LANES
     hbm = pl.BlockSpec(memory_space=pltpu.HBM)
     dma = pltpu.SemaphoreType.DMA
-    returned, grad_down, grad_up = pl.pallas_call(
+    results = pl.pallas_call(
         functools.partial(gather_kernel, sections, n, parts),
         out_shape=(
             jax.ShapeDtypeStruct((rows, width), jnp.bfloat16),
@@ -469,7 +478,7 @@
         out_specs=(hbm, hbm, hbm),
         scratch_shapes=[
             pltpu.VMEM((n, 2, rows, width), jnp.bfloat16),
-            pltpu.VMEM((n, rows + 8, 2 * WIDE), jnp.bfloat16),
+            pltpu.VMEM((n, rows, packed), jnp.bfloat16),
             pltpu.VMEM((WIDE, width), jnp.bfloat16),
             pltpu.VMEM((WIDE, width), jnp.bfloat16),
             pltpu.VMEM((rows, LANES), jnp.float32),
@@ -511,6 +520,14 @@
         recv_from,
         back_live,
     )
+    returned, grad_down, grad_up = pl.pallas_call(
+        place_kernel,
+        out_shape=[jax.ShapeDtypeStruct(r.shape, r.dtype) for r in results],
+        in_specs=[hbm] * 3,
+        out_specs=[hbm] * 3,
+        scratch_shapes=[dma((3, 3))],
+        compiler_params=pltpu.CompilerParams(vmem_limit_bytes=60 * 1024 * 1024),
+    )(*results)
     return returned.reshape(stash.shape), grad_down[None], grad_up[None]
 
 

time: 51.1 us -> 143 us (2.80)
  Pallas kernels: 44.1 us -> 141 us
  local copies, waits for them, and re-layouts: 5.46 us -> 0 us
    pallas_call x0 -> x1, Pallas kernels: none -> 98 us  [gathered(): pl.pallas_call(place_kernel, out_shape=[jax.ShapeDtypeStruct(r.shape, r.d...]
    unnamed x5 -> x0, local copies, waits for them, and re-layouts: 5.46 us -> none
where the time goes in v3:
time: 143 us
  Pallas kernels  141 us (99%)
    pallas_call x1, Pallas kernels, gathered(): pl.pallas_call(place_kernel, out_shape=[jax.ShapeDtypeStruct(r.shape, r.d...  98 us
    pallas_call x1, Pallas kernels, gathered(): pl.pallas_call(functools.partial(gather_kernel, sections, n, parts), out_...  43.4 us

profile of v3, /device:TPU:1, one launch (start us, length us, event | category | flops | bytes accessed | tf_op | source)
XLA Modules:
  0.0 142.6 jit_solution(16124243698663475240)
XLA Ops:
  1.3 43.4 %shard_map.112 = (bf16[24,5120]{1,0:T(8,128)(2,1)}, bf16[144,5120]{1,0:T(8,128)(2,1)}, bf16[144,5120]{1,0:T(8,128)(2,1)}) custom-call(bf16[24,5120]{1,0:T(8,128)(2,1)} %bitcast.9, bf16[24,5120]{1,0:T(8,128)(2,1)} %bitcast.10, bf16[144,5120]{1,0:T(8,128)(2,1)} %bitcast.7, bf16[144,5120]{1,0:T(8,128)(2,1)} %bitcast.8, f32[1,5120]{1,0:T(1,128)} %gain_in.1, ...), custom_call_target="tpu_custom_call" | custom-call | flops 707788800 | bytes 11796480 | tf_op jit(solution)/shard_map/pallas_call | solution.py:470
  44.6 98.0 %shard_map.113 = (bf16[24,5120]{1,0:T(8,128)(2,1)}, bf16[144,5120]{1,0:T(8,128)(2,1)}, bf16[144,5120]{1,0:T(8,128)(2,1)}) custom-call(bf16[24,5120]{1,0:T(8,128)(2,1)} %get-tuple-element.9.refs_0_, bf16[144,5120]{1,0:T(8,128)(2,1)} %get-tuple-element.10.refs_1_, bf16[144,5120]{1,0:T(8,128)(2,1)} %get-tuple-element.11.refs_2_), custom_call_target="tpu_custom_call" | custom-call | tf_op jit(solution)/shard_map/pallas_call | solution.py:523

commit v4 on v3

--- a/solution.py
+++ b/solution.py
@@ -444,18 +444,27 @@
 
 
 def place_kernel(*refs):
-    copies = []
-    for i in range(3):
-        source, target, sem = refs[i], refs[3 + i], refs[6]
-        height = source.shape[0]
+    sources, targets, held, (read_sem, write_sem) = refs[:3], refs[3:6], refs[6:9], refs[9:]
+    reads, writes = [], []
+    for i in (1, 2, 0):
+        height = sources[i].shape[0]
         pieces = 3 if height % 48 == 0 else 1
         for piece in range(pieces):
             span = pl.ds(piece * (height // pieces), height // pieces)
-            copies.append(pltpu.make_async_copy(source.at[span], target.at[span], sem.at[i, piece]))
-    for copy in copies:
-        copy.start()
-    for copy in copies:
-        copy.wait()
+            inside = held[i].at[span]
+            reads.append(
+                pltpu.make_async_copy(sources[i].at[span], inside, read_sem.at[i, piece])
+            )
+            writes.append(
+                pltpu.make_async_copy(inside, targets[i].at[span], write_sem.at[i, piece])
+            )
+    for read in reads:
+        read.start()
+    for read, write in zip(reads, writes):
+        read.wait()
+        write.start()
+    for write in writes:
+        write.wait()
 
 
 def gathered(stash, back_in, down_proj, up_proj, gain, sent_to, sent_count, recv_from, back_live):
@@ -525,7 +534,7 @@
         out_shape=[jax.ShapeDtypeStruct(r.shape, r.dtype) for r in results],
         in_specs=[hbm] * 3,
         out_specs=[hbm] * 3,
-        scratch_shapes=[dma((3, 3))],
+        scratch_shapes=[pltpu.VMEM(r.shape, r.dtype) for r in results] + [dma((3, 3))] * 2,
         compiler_params=pltpu.CompilerParams(vmem_limit_bytes=60 * 1024 * 1024),
     )(*results)
     return returned.reshape(stash.shape), grad_down[None], grad_up[None]

time: 143 us -> 47.7 us (0.33)
  Pallas kernels: 141 us -> 46.2 us
    pallas_call x1, Pallas kernels: 98 us -> 2.85 us  [gathered(): pl.pallas_call(place_kernel, out_shape=[jax.ShapeDtypeStruct(r.shape, r.d...]
where the time goes in v4:
time: 47.7 us; the launch traced here: 47.5 us
  Pallas kernels  46.2 us (97%)
  between operations  1.29 us (3%)
    pallas_call x1, Pallas kernels, gathered(): pl.pallas_call(functools.partial(gather_kernel, sections, n, parts), out_...  43.4 us
    pallas_call x1, Pallas kernels, gathered(): pl.pallas_call(place_kernel, out_shape=[jax.ShapeDtypeStruct(r.shape, r.d...  2.85 us

profile of v4, /device:TPU:1, one launch (start us, length us, event | category | flops | bytes accessed | tf_op | source)
XLA Modules:
  0.0 47.5 jit_solution(17932457057740372731)
XLA Ops:
  1.3 43.4 %shard_map.112 = (bf16[24,5120]{1,0:T(8,128)(2,1)}, bf16[144,5120]{1,0:T(8,128)(2,1)}, bf16[144,5120]{1,0:T(8,128)(2,1)}) custom-call(bf16[24,5120]{1,0:T(8,128)(2,1)} %bitcast.9, bf16[24,5120]{1,0:T(8,128)(2,1)} %bitcast.10, bf16[144,5120]{1,0:T(8,128)(2,1)} %bitcast.7, bf16[144,5120]{1,0:T(8,128)(2,1)} %bitcast.8, f32[1,5120]{1,0:T(1,128)} %gain_in.1, ...), custom_call_target="tpu_custom_call" | custom-call | flops 707788800 | bytes 11796480 | tf_op jit(solution)/shard_map/pallas_call | solution.py:479
  44.6 2.9 %shard_map.113 = (bf16[24,5120]{1,0:T(8,128)(2,1)}, bf16[144,5120]{1,0:T(8,128)(2,1)}, bf16[144,5120]{1,0:T(8,128)(2,1)}) custom-call(bf16[24,5120]{1,0:T(8,128)(2,1)} %get-tuple-element.9.refs_0_, bf16[144,5120]{1,0:T(8,128)(2,1)} %get-tuple-element.10.refs_1_, bf16[144,5120]{1,0:T(8,128)(2,1)} %get-tuple-element.11.refs_2_), custom_call_target="tpu_custom_call" | custom-call | tf_op jit(solution)/shard_map/pallas_call | solution.py:532

commit v5 on v4

--- a/solution.py
+++ b/solution.py
@@ -237,16 +237,20 @@
     def _():
         pl.semaphore_wait(barrier, 3)
 
-    for j in range(parts):
+    def send_own(j, carry):
         for kind in (0, 1):
 
             @pl.when(has_right)
-            def _(j=j, kind=kind):
+            def _(kind=kind):
                 along(me, kind, j, 1, True).start()
 
             @pl.when(has_left)
-            def _(j=j, kind=kind):
+            def _(kind=kind):
                 along(me, kind, j, -1, True).start()
+
+        return carry
+
+    lax.fori_loop(0, parts, send_own, 0)
 
     for load in small:
         load.wait()
@@ -354,12 +358,15 @@
                 def _():
                     factor_along(origin, step).start()
 
+    def pass_on(distance, j, carry):
+        arrivals(distance, j)
+        return carry
+
     for distance in range(1, n):
         arrivals(distance, 0)
         factor_arrivals(distance)
         if distance < n - 1:
-            for j in range(1, parts):
-                arrivals(distance, j)
+            lax.fori_loop(1, parts, functools.partial(pass_on, distance), 0)
 
     want_copy().wait()
     body_all = jnp.concatenate([factors[a].astype(jnp.float32) for a in range(n)], axis=0)
@@ -472,7 +479,7 @@
     slots, micro, width = stash.shape[2:]
     rows = slots * micro
     rank = down_proj.shape[1]
-    parts = 4
+    parts = 10
     packed = -(-(2 * rank + 3) // LANES) * LANES
     hbm = pl.BlockSpec(memory_space=pltpu.HBM)
     dma = pltpu.SemaphoreType.DMA

time: 47.7 us -> 49.4 us (1.036)
  Pallas kernels: 46.2 us -> 48 us
    pallas_call x1, Pallas kernels: 43.4 us -> 45.1 us  [gathered(): pl.pallas_call(functools.partial(gather_kernel, sections, n, parts), out_...]
where the time goes in v5:
time: 49.4 us; the launch traced here: 49.3 us
  Pallas kernels  48 us (97%)
  between operations  1.29 us (3%)
    pallas_call x1, Pallas kernels, gathered(): pl.pallas_call(functools.partial(gather_kernel, sections, n, parts), out_...  45.1 us
    pallas_call x1, Pallas kernels, gathered(): pl.pallas_call(place_kernel, out_shape=[jax.ShapeDtypeStruct(r.shape, r.d...  2.85 us

profile of v5, /device:TPU:1, one launch (start us, length us, event | category | flops | bytes accessed | tf_op | source)
XLA Modules:
  0.0 49.3 jit_solution(68799428784896350)
XLA Ops:
  1.3 45.1 %shard_map.112 = (bf16[24,5120]{1,0:T(8,128)(2,1)}, bf16[144,5120]{1,0:T(8,128)(2,1)}, bf16[144,5120]{1,0:T(8,128)(2,1)}) custom-call(bf16[24,5120]{1,0:T(8,128)(2,1)} %bitcast.9, bf16[24,5120]{1,0:T(8,128)(2,1)} %bitcast.10, bf16[144,5120]{1,0:T(8,128)(2,1)} %bitcast.7, bf16[144,5120]{1,0:T(8,128)(2,1)} %bitcast.8, f32[1,5120]{1,0:T(1,128)} %gain_in.1, ...), custom_call_target="tpu_custom_call" | custom-call | flops 707788800 | bytes 11796480 | tf_op jit(solution)/shard_map/pallas_call | solution.py:486
  46.4 2.9 %shard_map.113 = (bf16[24,5120]{1,0:T(8,128)(2,1)}, bf16[144,5120]{1,0:T(8,128)(2,1)}, bf16[144,5120]{1,0:T(8,128)(2,1)}) custom-call(bf16[24,5120]{1,0:T(8,128)(2,1)} %get-tuple-element.9.refs_0_, bf16[144,5120]{1,0:T(8,128)(2,1)} %get-tuple-element.10.refs_1_, bf16[144,5120]{1,0:T(8,128)(2,1)} %get-tuple-element.11.refs_2_), custom_call_target="tpu_custom_call" | custom-call | tf_op jit(solution)/shard_map/pallas_call | solution.py:539

commit v6 on v4

--- a/solution.py
+++ b/solution.py
@@ -143,10 +143,17 @@
     after = lax.rem(section + 1, sections)
     rows, width = stash.shape
     rank = down.shape[0]
-    part = width // parts
+    even = 4
+    part = width // even
+    narrow = width // (10 * LANES) * LANES
+    wide = (width - narrow) // (parts - 1) // LANES * LANES
+    sizes = [wide] * (parts - 1) + [width - wide * (parts - 1)]
     has_left, has_right = me > 0, me < n - 1
 
     def cols(j):
+        return pl.ds(j * wide, sizes[j])
+
+    def even_cols(j):
         return pl.ds(pl.multiple_of(j * part, part), part)
 
     def along(origin, kind, j, step, own=False):
@@ -271,30 +278,30 @@
         load.wait()
 
     def square_part(j, total):
-        block = rows_all[me, 0, :, cols(j)].astype(jnp.float32)
+        block = rows_all[me, 0, :, even_cols(j)].astype(jnp.float32)
         return total + jnp.sum(block * block, axis=-1, keepdims=True)
 
-    squares = lax.fori_loop(0, parts, square_part, jnp.zeros((rows, 1), jnp.float32))
+    squares = lax.fori_loop(0, even, square_part, jnp.zeros((rows, 1), jnp.float32))
     inverse = lax.rsqrt(squares / width + epsilon)
     contract_last = (((1,), (1,)), ((), ()))
 
     def project_part(j, carry):
         pre, back = carry
-        block = rows_all[me, 0, :, cols(j)].astype(jnp.float32)
-        normed = (block * inverse * gain_ref[:, cols(j)]).astype(jnp.bfloat16)
+        block = rows_all[me, 0, :, even_cols(j)].astype(jnp.float32)
+        normed = (block * inverse * gain_ref[:, even_cols(j)]).astype(jnp.bfloat16)
         pre = pre + lax.dot_general(
-            normed, w_down[:, cols(j)], contract_last, preferred_element_type=jnp.float32
+            normed, w_down[:, even_cols(j)], contract_last, preferred_element_type=jnp.float32
         )
         back = back + lax.dot_general(
-            rows_all[me, 1, :, cols(j)],
-            w_up[:, cols(j)],
+            rows_all[me, 1, :, even_cols(j)],
+            w_up[:, even_cols(j)],
             contract_last,
             preferred_element_type=jnp.float32,
         )
         return pre, back
 
     empty = jnp.zeros((rows, WIDE), jnp.float32)
-    preact, back_act = lax.fori_loop(0, parts, project_part, (empty, empty))
+    preact, back_act = lax.fori_loop(0, even, project_part, (empty, empty))
     row_only = lax.broadcasted_iota(jnp.int32, (rows, 1), 0)
     live = jnp.zeros((rows, 1), jnp.float32)
     code = jnp.zeros((rows, 1), jnp.float32)
@@ -376,9 +383,8 @@
     down_pick = jnp.concatenate([select, body_t[:rank]], axis=0).astype(jnp.bfloat16)
     up_pick = jnp.concatenate([select, body_t[rank : 2 * rank]], axis=0).astype(jnp.bfloat16)
 
-    def finish(j, carry):
-        @pl.when(j > 0)
-        def _():
+    def finish(j):
+        if j > 0:
             arrivals(n - 1, j)
 
         gain = gain_ref[:, cols(j)]
@@ -398,11 +404,11 @@
         grad_up[:, cols(j)] = (from_back[rows:] / n).astype(jnp.bfloat16)
         for store in stores(j):
             store.start()
-        return carry
-
-    lax.fori_loop(0, parts, finish, 0)
-
-    def drain(j, carry):
+
+    for j in range(parts):
+        finish(j)
+
+    def drain(j):
         back_copy(j).wait()
         for store in stores(j):
             store.wait()
@@ -427,9 +433,8 @@
                     for kind in (0, 1):
                         along(origin, kind, j, step).wait_send()
 
-        return carry
-
-    lax.fori_loop(0, parts, drain, 0)
+    for j in range(parts):
+        drain(j)
 
     for distance in range(n):
         for step in (1, -1):

time: 47.7 us -> 47.6 us (level)
  no operation moved by 1% of the time
where the time goes in v6:
time: 47.6 us; the launch traced here: 47.4 us
  Pallas kernels  46.2 us (97%)
  between operations  1.29 us (3%)
    pallas_call x1, Pallas kernels, gathered(): pl.pallas_call(functools.partial(gather_kernel, sections, n, parts), out_...  43.3 us
    pallas_call x1, Pallas kernels, gathered(): pl.pallas_call(place_kernel, out_shape=[jax.ShapeDtypeStruct(r.shape, r.d...  2.85 us

profile of v6, /device:TPU:1, one launch (start us, length us, event | category | flops | bytes accessed | tf_op | source)
XLA Modules:
  0.0 47.4 jit_solution(8605629999334165699)
XLA Ops:
  1.3 43.3 %shard_map.112 = (bf16[24,5120]{1,0:T(8,128)(2,1)}, bf16[144,5120]{1,0:T(8,128)(2,1)}, bf16[144,5120]{1,0:T(8,128)(2,1)}) custom-call(bf16[24,5120]{1,0:T(8,128)(2,1)} %bitcast.9, bf16[24,5120]{1,0:T(8,128)(2,1)} %bitcast.10, bf16[144,5120]{1,0:T(8,128)(2,1)} %bitcast.7, bf16[144,5120]{1,0:T(8,128)(2,1)} %bitcast.8, f32[1,5120]{1,0:T(1,128)} %gain_in.1, ...), custom_call_target="tpu_custom_call" | custom-call | flops 707788800 | bytes 11796480 | tf_op jit(solution)/shard_map/pallas_call | solution.py:484
  44.6 2.9 %shard_map.113 = (bf16[24,5120]{1,0:T(8,128)(2,1)}, bf16[144,5120]{1,0:T(8,128)(2,1)}, bf16[144,5120]{1,0:T(8,128)(2,1)}) custom-call(bf16[24,5120]{1,0:T(8,128)(2,1)} %get-tuple-element.9.refs_0_, bf16[144,5120]{1,0:T(8,128)(2,1)} %get-tuple-element.10.refs_1_, bf16[144,5120]{1,0:T(8,128)(2,1)} %get-tuple-element.11.refs_2_), custom_call_target="tpu_custom_call" | custom-call | tf_op jit(solution)/shard_map/pallas_call | solution.py:537

commit v7 on v6

--- a/solution.py
+++ b/solution.py
@@ -477,7 +477,7 @@
     slots, micro, width = stash.shape[2:]
     rows = slots * micro
     rank = down_proj.shape[1]
-    parts = 4
+    parts = 3
     packed = -(-(2 * rank + 3) // LANES) * LANES
     hbm = pl.BlockSpec(memory_space=pltpu.HBM)
     dma = pltpu.SemaphoreType.DMA

time: 47.6 us -> 48 us (level)
  no operation moved by 1% of the time
where the time goes in v7:
time: 48 us; the launch traced here: 47.8 us
  Pallas kernels  46.5 us (97%)
  between operations  1.29 us (3%)
    pallas_call x1, Pallas kernels, gathered(): pl.pallas_call(functools.partial(gather_kernel, sections, n, parts), out_...  43.7 us
    pallas_call x1, Pallas kernels, gathered(): pl.pallas_call(place_kernel, out_shape=[jax.ShapeDtypeStruct(r.shape, r.d...  2.85 us

profile of v7, /device:TPU:1, one launch (start us, length us, event | category | flops | bytes accessed | tf_op | source)
XLA Modules:
  0.0 47.8 jit_solution(1439121999783969222)
XLA Ops:
  1.3 43.7 %shard_map.112 = (bf16[24,5120]{1,0:T(8,128)(2,1)}, bf16[144,5120]{1,0:T(8,128)(2,1)}, bf16[144,5120]{1,0:T(8,128)(2,1)}) custom-call(bf16[24,5120]{1,0:T(8,128)(2,1)} %bitcast.9, bf16[24,5120]{1,0:T(8,128)(2,1)} %bitcast.10, bf16[144,5120]{1,0:T(8,128)(2,1)} %bitcast.7, bf16[144,5120]{1,0:T(8,128)(2,1)} %bitcast.8, f32[1,5120]{1,0:T(1,128)} %gain_in.1, ...), custom_call_target="tpu_custom_call" | custom-call | flops 707788800 | bytes 11796480 | tf_op jit(solution)/shard_map/pallas_call | solution.py:484
  45.0 2.9 %shard_map.113 = (bf16[24,5120]{1,0:T(8,128)(2,1)}, bf16[144,5120]{1,0:T(8,128)(2,1)}, bf16[144,5120]{1,0:T(8,128)(2,1)}) custom-call(bf16[24,5120]{1,0:T(8,128)(2,1)} %get-tuple-element.9.refs_0_, bf16[144,5120]{1,0:T(8,128)(2,1)} %get-tuple-element.10.refs_1_, bf16[144,5120]{1,0:T(8,128)(2,1)} %get-tuple-element.11.refs_2_), custom_call_target="tpu_custom_call" | custom-call | tf_op jit(solution)/shard_map/pallas_call | solution.py:537
